TPU v7x, 32 devices: a whole 2x2x4 slice. The times are simulated.
32 devices in a mesh: grp: 2 (over x), wide: 16 (over z, y, core).
Axes of the slice: x: 2, y: 2, z: 4, core: 2. Of those that a mesh axis runs over, the one named last changes fastest.
Arguments:
- activations: bfloat16 [128, 2, 32, 4096], P(('grp', 'wide')), parts along dimension 0, may hold values from -6 to 6
- out_grads: bfloat16 [128, 2, 32, 4096], P(('grp', 'wide')), parts along dimension 0, may hold values from -6 to 6
- lengths: int32 [128], P(('grp', 'wide')), parts along dimension 0, may hold values from 1 to 32, as said below
- proj_in: bfloat16 [2, 4096, 128], replicated
- proj_out: bfloat16 [2, 4096, 256], replicated
Outputs:
- precond: bfloat16 [128, 65536], P(('grp', 'wide')), parts along dimension 0
There are 2 independent parts, one for each index of `grp`. A program takes and returns all parts, laid end to end along the dimension named above; an argument that names none is the same for every part. Nothing has to cross between parts.
Inputs may be any that keep to these rules, and one draw needn't show every extreme that they name: `lengths`: some sequence of every group has all 32 tokens valid.
All inputs are finite; a program needn't handle non-finite values.
Results may differ from a plain program's by a relative error of at most 0.0061.
Values may be sent and summed in bfloat16 or wider, within the bound.
A program may use at most 64 MiB of HBM per device.

v0:
```python
import functools
import math

import jax
import jax.numpy as jnp
from jax import lax
from jax.experimental import pallas as pl
from jax.experimental.pallas import tpu as pltpu
from jax.sharding import PartitionSpec as P

BLOCK = 512
NS_ITERS = 5
DAMPING = 0.1
CHUNKS = 2
MESH = pl.DeviceIdType.MESH


def precondition(rows):
    row_count = rows.shape[0]
    order = rows.shape[2]
    highest = lax.Precision.HIGHEST
    identity = jnp.eye(row_count, dtype=jnp.float32)[None]
    gram = jnp.einsum("ska,tka->kst", rows, rows, preferred_element_type=jnp.float32) / row_count
    trace_sum = jnp.trace(gram, axis1=1, axis2=2)[:, None, None]
    damping = DAMPING * trace_sum / order
    squares = jnp.sum(gram * gram, axis=(1, 2), keepdims=True)
    frobenius = jnp.sqrt(squares + 2.0 * damping * trace_sum + order * damping * damping)
    power = identity - (gram + damping * identity) / frobenius
    total = identity + power
    for _ in range(NS_ITERS - 1):
        power = jnp.einsum("kab,kbc->kac", power, power, precision=highest)
        total = total + jnp.einsum("kab,kbc->kac", total, power, precision=highest)
    return jnp.einsum(
        "kst,tka->ska", total / frobenius, rows.astype(jnp.float32), precision=highest
    ).astype(jnp.bfloat16)


def local_plain(activations, out_grads, lengths, proj_in, proj_out):
    seq_count, module_count, seq_len, model_width = activations.shape
    rank_in = proj_in.shape[2]
    rank_out = proj_out.shape[2]
    acc_in = jnp.einsum("smtd,mdr->smtr", activations, proj_in, preferred_element_type=jnp.float32)
    acc_out = jnp.einsum("smtd,mdr->smtr", out_grads, proj_out, preferred_element_type=jnp.float32)
    positions = lax.broadcasted_iota(jnp.int32, (seq_count, seq_len), 1)
    valid_mask = (positions < lengths[:, None]).astype(jnp.float32)[:, None, :, None]
    projected_in = (acc_in * valid_mask).astype(jnp.bfloat16)
    projected_out = (acc_out * valid_mask).astype(jnp.bfloat16)
    seq_grads = jnp.einsum(
        "smto,smti->smoi", projected_out, projected_in, preferred_element_type=jnp.float32
    ) * (1.0 / math.sqrt(seq_len))
    grad_size = module_count * rank_out * rank_in
    wide_count = lax.axis_size("wide")
    blocks_here = grad_size // (BLOCK * wide_count)
    blocks = seq_grads.astype(jnp.bfloat16).reshape(seq_count, wide_count, blocks_here, BLOCK)
    owned_rows = lax.all_to_all(blocks, "wide", split_axis=1, concat_axis=0, tiled=True)
    result = precondition(owned_rows[:, 0])[:, None]
    returned = lax.all_to_all(result, "wide", split_axis=0, concat_axis=1, tiled=True)
    return returned.reshape(seq_count, grad_size)


def split_dot(left, right):
    left_high = left.astype(jnp.bfloat16)
    left_low = (left - left_high.astype(jnp.float32)).astype(jnp.bfloat16)
    right_high = right.astype(jnp.bfloat16)
    right_low = (right - right_high.astype(jnp.float32)).astype(jnp.bfloat16)
    dot = functools.partial(jnp.dot, preferred_element_type=jnp.float32)
    return dot(left_high, right_high) + (dot(left_high, right_low) + dot(left_low, right_high))


def polynomial(stacked, group, order, row_count):
    size = stacked.shape[0]
    row = lax.broadcasted_iota(jnp.int32, (size, size), 0)
    column = lax.broadcasted_iota(jnp.int32, (size, size), 1)
    same = jnp.where(row // row_count == column // row_count, 1.0, 0.0).astype(jnp.float32)
    identity = jnp.where(row == column, 1.0, 0.0).astype(jnp.float32)
    gram = lax.dot_general(
        stacked, stacked, (((1,), (1,)), ((), ())), preferred_element_type=jnp.float32
    )
    gram = jnp.where(row // row_count == column // row_count, gram, 0.0) * (1.0 / row_count)
    diagonal = jnp.sum(gram * identity, axis=0, keepdims=True)
    trace_sum = jnp.sum(same * diagonal, axis=1, keepdims=True)
    squares = jnp.sum(gram * gram, axis=0, keepdims=True)
    squares = jnp.sum(same * squares, axis=1, keepdims=True)
    damping = (DAMPING / order) * trace_sum
    frobenius = jnp.sqrt(squares + 2.0 * damping * trace_sum + order * damping * damping)
    scale = 1.0 / frobenius
    power = identity - (gram + damping * identity) * scale
    total = identity + power
    for _ in range(NS_ITERS - 1):
        power = split_dot(power, power)
        total = total + split_dot(total, power)
    return total * scale


def kernel(
    wide, lengths_ref, act_ref, grad_ref, in_ref, out_proj_ref, result_ref,
    act_v, grad_v, in_v, out_v, outgoing, rows_v, work, finished,
    load_sem, send_sem, recv_sem, back_send_sem, back_recv_sem,
):
    seqs, modules, seq_len, width = act_ref.shape
    rank_in = in_ref.shape[2]
    rank_out = out_proj_ref.shape[2]
    here = rank_out // wide
    all_seqs = seqs * wide
    lanes = BLOCK // rank_in
    blocks = here // lanes
    depth = width // CHUNKS
    me = lax.axis_index("wide")

    def loads(m, c):
        span = pl.ds(c * depth, depth)
        return (
            pltpu.make_async_copy(act_ref.at[:, m, :, span], act_v.at[m, c], load_sem.at[m, c, 0]),
            pltpu.make_async_copy(in_ref.at[m, span, :], in_v.at[m, c], load_sem.at[m, c, 1]),
            pltpu.make_async_copy(grad_ref.at[:, m, :, span], grad_v.at[m, c], load_sem.at[m, c, 2]),
            pltpu.make_async_copy(out_proj_ref.at[m, span, :], out_v.at[m, c], load_sem.at[m, c, 3]),
        )

    for m in range(modules):
        for c in range(CHUNKS):
            for copy in loads(m, c):
                copy.start()

    barrier = pltpu.get_barrier_semaphore()

    def greet(d, carry):
        pl.semaphore_signal(
            barrier, inc=1, device_id={"wide": lax.rem(me + d, wide)}, device_id_type=MESH
        )
        return carry

    lax.fori_loop(1, wide, greet, 0)

    def scatter(m, d):
        target = lax.rem(me + d, wide)
        return pltpu.make_async_remote_copy(
            src_ref=outgoing.at[m, target],
            dst_ref=rows_v.at[m, pl.ds(me * seqs, seqs)],
            send_sem=send_sem.at[m, d],
            recv_sem=recv_sem.at[m, d],
            device_id={"wide": target},
            device_id_type=MESH,
        )

    def give_back(m, d):
        target = lax.rem(me + d, wide)
        return pltpu.make_async_remote_copy(
            src_ref=finished.at[m, pl.ds(target * seqs, seqs)],
            dst_ref=result_ref.at[:, m, pl.ds(pl.multiple_of(me * here, here), here), :],
            send_sem=back_send_sem.at[m, d],
            recv_sem=back_recv_sem.at[m, d],
            device_id={"wide": target},
            device_id_type=MESH,
        )

    def each(action):
        def body(d, carry):
            action(d)
            return carry

        lax.fori_loop(1, wide, body, 0)

    dot = functools.partial(jnp.dot, preferred_element_type=jnp.float32)
    positions = lax.broadcasted_iota(jnp.int32, (seq_len, 1), 0)
    for m in range(modules):
        acc_in = jnp.zeros((seqs * seq_len, rank_in), jnp.float32)
        acc_out = jnp.zeros((seqs * seq_len, rank_out), jnp.float32)
        for c in range(CHUNKS):
            for copy in loads(m, c):
                copy.wait()
            acc_in = acc_in + dot(act_v[m, c].reshape(seqs * seq_len, depth), in_v[m, c])
            acc_out = acc_out + dot(grad_v[m, c].reshape(seqs * seq_len, depth), out_v[m, c])
        for s in range(seqs):
            valid = jnp.where(positions < lengths_ref[s], 1.0, 0.0).astype(jnp.float32)
            part = slice(s * seq_len, (s + 1) * seq_len)
            left = (acc_out[part] * valid).astype(jnp.bfloat16)
            right = (acc_in[part] * valid).astype(jnp.bfloat16)
            product = lax.dot_general(
                left, right, (((0,), (0,)), ((), ())), preferred_element_type=jnp.float32
            ) * (1.0 / math.sqrt(seq_len))
            outgoing[m, :, s] = product.astype(jnp.bfloat16).reshape(wide, here, rank_in)
        if m == 0:
            pl.semaphore_wait(barrier, wide - 1)
        each(lambda d: scatter(m, d).start())
        rows_v[m, pl.ds(me * seqs, seqs)] = outgoing[m, me]

    for m in range(modules):
        each(lambda d: scatter(m, d).wait_recv())
        work[...] = rows_v[m].astype(jnp.float32).reshape(all_seqs * here, rank_in)
        stacked = jnp.concatenate(
            [
                jnp.concatenate(
                    [
                        work[pl.ds(b * lanes + j, all_seqs, stride=here), :].astype(jnp.bfloat16)
                        for j in range(lanes)
                    ],
                    axis=1,
                )
                for b in range(blocks)
            ],
            axis=0,
        )
        inverse = polynomial(stacked, blocks, BLOCK, all_seqs)
        high = inverse.astype(jnp.bfloat16)
        low = (inverse - high.astype(jnp.float32)).astype(jnp.bfloat16)
        solved = dot(high, stacked) + dot(low, stacked)
        for b in range(blocks):
            for j in range(lanes):
                work[pl.ds(b * lanes + j, all_seqs, stride=here), :] = solved[
                    b * all_seqs : (b + 1) * all_seqs, j * rank_in : (j + 1) * rank_in
                ]
        finished[m] = work[...].astype(jnp.bfloat16).reshape(all_seqs, here, rank_in)
        each(lambda d: give_back(m, d).start())
        result_ref[:, m, pl.ds(pl.multiple_of(me * here, here), here), :] = finished[
            m, pl.ds(me * seqs, seqs)
        ]

    for m in range(modules):
        each(lambda d: scatter(m, d).wait_send())
        each(lambda d: give_back(m, d).wait_recv())
        each(lambda d: give_back(m, d).wait_send())


def local_fused(wide, activations, out_grads, lengths, proj_in, proj_out):
    seqs, modules, seq_len, width = activations.shape
    rank_in = proj_in.shape[2]
    rank_out = proj_out.shape[2]
    here = rank_out // wide
    depth = width // CHUNKS
    all_seqs = seqs * wide
    any_spec = pl.BlockSpec(memory_space=pl.ANY)
    bf16 = jnp.bfloat16
    out = pl.pallas_call(
        functools.partial(kernel, wide),
        out_shape=jax.ShapeDtypeStruct((seqs, modules, rank_out, rank_in), bf16),
        in_specs=[pl.BlockSpec(memory_space=pltpu.SMEM)] + [any_spec] * 4,
        out_specs=pl.BlockSpec(memory_space=pltpu.VMEM),
        scratch_shapes=[
            pltpu.VMEM((modules, CHUNKS, seqs, seq_len, depth), bf16),
            pltpu.VMEM((modules, CHUNKS, seqs, seq_len, depth), bf16),
            pltpu.VMEM((modules, CHUNKS, depth, rank_in), bf16),
            pltpu.VMEM((modules, CHUNKS, depth, rank_out), bf16),
            pltpu.VMEM((modules, wide, seqs, here, rank_in), bf16),
            pltpu.VMEM((modules, all_seqs, here, rank_in), bf16),
            pltpu.VMEM((all_seqs * here, rank_in), jnp.float32),
            pltpu.VMEM((modules, all_seqs, here, rank_in), bf16),
            pltpu.SemaphoreType.DMA((modules, CHUNKS, 4)),
            pltpu.SemaphoreType.DMA((modules, wide)),
            pltpu.SemaphoreType.DMA((modules, wide)),
            pltpu.SemaphoreType.DMA((modules, wide)),
            pltpu.SemaphoreType.DMA((modules, wide)),
        ],
        compiler_params=pltpu.CompilerParams(
            collective_id=0, has_side_effects=True, vmem_limit_bytes=40 * 1024 * 1024
        ),
    )(lengths, activations, out_grads, proj_in, proj_out)
    return out.reshape(seqs, modules * rank_out * rank_in)


def solution(mesh):
    in_specs = (
        P(("grp", "wide"), None, None, None),
        P(("grp", "wide"), None, None, None),
        P(("grp", "wide")),
        P(),
        P(),
    )
    out_specs = P(("grp", "wide"), None)
    wide = mesh.shape["wide"]

    def local(activations, out_grads, lengths, proj_in, proj_out):
        here = proj_out.shape[2] // wide
        lanes = BLOCK // proj_in.shape[2]
        stacked = activations.shape[0] * wide * max(here // lanes, 1)
        if here % 16 == 0 and here % lanes == 0 and stacked <= 512:
            return local_fused(wide, activations, out_grads, lengths, proj_in, proj_out)
        return local_plain(activations, out_grads, lengths, proj_in, proj_out)

    return jax.shard_map(
        local, mesh=mesh, in_specs=in_specs, out_specs=out_specs, check_vma=False
    )
```

profile of v0, /device:TPU:0, one launch (start us, length us, event | category | flops | bytes accessed | tf_op | source)
XLA Modules:
  0.0 40.9 jit_solution(4547399622030031205)
XLA Ops:
  0.0 0.0 copy-start
  0.0 2.2 %copy-done = bf16[2,4096,256]{2,1,0:T(8,128)(2,1)S(1)} copy-done((bf16[2,4096,256]{2,1,0:T(8,128)(2,1)S(1)}, bf16[2,4096,256]{2,1,0:T(8,128)(2,1)}, u32[]{:S(2)}) %copy-start) | copy-done | bytes 4194328
  2.2 0.0 copy-start.1
  2.2 1.6 %copy-done.1 = bf16[4,2,32,4096]{3,2,1,0:T(8,128)(2,1)S(1)} copy-done((bf16[4,2,32,4096]{3,2,1,0:T(8,128)(2,1)S(1)}, bf16[4,2,32,4096]{3,2,1,0:T(8,128)(2,1)}, u32[]{:S(2)}) %copy-start.1) | copy-done | bytes 2097176
  3.8 0.0 copy-start.2
  3.8 1.6 %copy-done.2 = bf16[4,2,32,4096]{3,2,1,0:T(8,128)(2,1)S(1)} copy-done((bf16[4,2,32,4096]{3,2,1,0:T(8,128)(2,1)S(1)}, bf16[4,2,32,4096]{3,2,1,0:T(8,128)(2,1)}, u32[]{:S(2)}) %copy-start.2) | copy-done | bytes 2097176
  5.4 0.0 copy-start.3
  5.4 1.6 %copy-done.3 = bf16[2,4096,128]{2,1,0:T(8,128)(2,1)S(1)} copy-done((bf16[2,4096,128]{2,1,0:T(8,128)(2,1)S(1)}, bf16[2,4096,128]{2,1,0:T(8,128)(2,1)}, u32[]{:S(2)}) %copy-start.3) | copy-done | bytes 2097176
  7.0 0.0 copy-start.4
  7.0 0.7 %copy-done.4 = s32[4]{0:T(128)S(1)} copy-done((s32[4]{0:T(128)S(1)}, s32[4]{0:T(128)}, u32[]{:S(2)}) %copy-start.4) | copy-done | bytes 40
  7.6 32.0 %shard_map.55 = bf16[4,2,256,128]{3,2,1,0:T(8,128)(2,1)S(1)} custom-call(s32[4]{0:T(128)S(1)} %copy-done.4, bf16[4,2,32,4096]{3,2,1,0:T(8,128)(2,1)S(1)} %copy-done.1, bf16[4,2,32,4096]{3,2,1,0:T(8,128)(2,1)S(1)} %copy-done.2, bf16[2,4096,128]{2,1,0:T(8,128)(2,1)S(1)} %copy-done.3, bf16[2,4096,256]{2,1,0:T(8,128)(2,1)S(1)} %copy-done), custom_call_target="tpu_custom_call" | custom-call | tf_op jit(solution)/shard_map/pallas_call | solution.py:233
  39.7 1.2 %copy.8 = bf16[1,4,512,128]{3,1,2,0:T(4,128)(2,1)} copy(bf16[1,4,512,128]{3,2,1,0:T(8,128)(2,1)S(1)} %bitcast.5) | data formatting | bytes 1048576
Async XLA Ops:
  0.0 2.2 %copy-start = (bf16[2,4096,256]{2,1,0:T(8,128)(2,1)S(1)}, bf16[2,4096,256]{2,1,0:T(8,128)(2,1)}, u32[]{:S(2)}) copy-start(bf16[2,4096,256]{2,1,0:T(8,128)(2,1)} %out_proj_ref.1) | copy-start | bytes 12582916
  2.2 1.6 %copy-start.1 = (bf16[4,2,32,4096]{3,2,1,0:T(8,128)(2,1)S(1)}, bf16[4,2,32,4096]{3,2,1,0:T(8,128)(2,1)}, u32[]{:S(2)}) copy-start(bf16[4,2,32,4096]{3,2,1,0:T(8,128)(2,1)} %act_ref.1) | copy-start | bytes 6291460
  3.8 1.6 %copy-start.2 = (bf16[4,2,32,4096]{3,2,1,0:T(8,128)(2,1)S(1)}, bf16[4,2,32,4096]{3,2,1,0:T(8,128)(2,1)}, u32[]{:S(2)}) copy-start(bf16[4,2,32,4096]{3,2,1,0:T(8,128)(2,1)} %grad_ref.1) | copy-start | bytes 6291460
  5.4 1.6 %copy-start.3 = (bf16[2,4096,128]{2,1,0:T(8,128)(2,1)S(1)}, bf16[2,4096,128]{2,1,0:T(8,128)(2,1)}, u32[]{:S(2)}) copy-start(bf16[2,4096,128]{2,1,0:T(8,128)(2,1)} %in_ref.1) | copy-start | bytes 6291460
  7.0 0.7 %copy-start.4 = (s32[4]{0:T(128)S(1)}, s32[4]{0:T(128)}, u32[]{:S(2)}) copy-start(s32[4]{0:T(128)} %lengths_ref.1) | copy-start | bytes 52
where the time goes:
time: 41.1 us; the launch traced here: 40.9 us
  Pallas kernels  32 us (78%)
  local copies, waits for them, and re-layouts  8.81 us (21%)
    pallas_call x1, Pallas kernels, local_fused(): pl.pallas_call(functools.partial(kernel, wide), out_shape=jax.ShapeDtypeS...  32 us
    unnamed x11, local copies, waits for them, and re-layouts  8.81 us

commit v1 on v0

--- a/solution.py
+++ b/solution.py
@@ -58,38 +58,74 @@
     return returned.reshape(seq_count, grad_size)
 
 
-def split_dot(left, right):
-    left_high = left.astype(jnp.bfloat16)
-    left_low = (left - left_high.astype(jnp.float32)).astype(jnp.bfloat16)
-    right_high = right.astype(jnp.bfloat16)
-    right_low = (right - right_high.astype(jnp.float32)).astype(jnp.bfloat16)
-    dot = functools.partial(jnp.dot, preferred_element_type=jnp.float32)
-    return dot(left_high, right_high) + (dot(left_high, right_low) + dot(left_low, right_high))
-
-
-def polynomial(stacked, group, order, row_count):
+def polynomial(stacked, order, row_count):
     size = stacked.shape[0]
+    blocks = size // row_count
     row = lax.broadcasted_iota(jnp.int32, (size, size), 0)
     column = lax.broadcasted_iota(jnp.int32, (size, size), 1)
-    same = jnp.where(row // row_count == column // row_count, 1.0, 0.0).astype(jnp.float32)
-    identity = jnp.where(row == column, 1.0, 0.0).astype(jnp.float32)
+    same = row // row_count == column // row_count
+    short = (row_count, size)
+    lane = lax.broadcasted_iota(jnp.int32, (1, size), 1)
+    on_diagonal = (
+        lax.broadcasted_iota(jnp.int32, short, 0)
+        == lax.broadcasted_iota(jnp.int32, short, 1) % row_count
+    )
+    identity = jnp.where(on_diagonal, 1.0, 0.0).astype(jnp.float32)
+
+    def spread(beside):
+        tall = jnp.concatenate([beside] * blocks, axis=0)
+        return jnp.where(same, tall, 0.0).astype(jnp.bfloat16)
+
+    def halves(beside):
+        high = beside.astype(jnp.bfloat16).astype(jnp.float32)
+        return high, beside - high
+
+    def per_block(values):
+        total = jnp.zeros((1, size), jnp.float32)
+        for b in range(blocks):
+            mine = lane // row_count == b
+            part = jnp.sum(jnp.where(mine, values, 0.0), axis=1, keepdims=True)
+            total = jnp.where(mine, part, total)
+        return total
+
+    dot = functools.partial(jnp.dot, preferred_element_type=jnp.float32)
     gram = lax.dot_general(
         stacked, stacked, (((1,), (1,)), ((), ())), preferred_element_type=jnp.float32
     )
-    gram = jnp.where(row // row_count == column // row_count, gram, 0.0) * (1.0 / row_count)
-    diagonal = jnp.sum(gram * identity, axis=0, keepdims=True)
-    trace_sum = jnp.sum(same * diagonal, axis=1, keepdims=True)
-    squares = jnp.sum(gram * gram, axis=0, keepdims=True)
-    squares = jnp.sum(same * squares, axis=1, keepdims=True)
+    gram = jnp.where(same, gram, 0.0)
+    beside = gram[:row_count]
+    for b in range(1, blocks):
+        beside = beside + gram[b * row_count : (b + 1) * row_count]
+    beside = beside * (1.0 / row_count)
+    trace_sum = per_block(jnp.sum(beside * identity, axis=0, keepdims=True))
+    squares = per_block(jnp.sum(beside * beside, axis=0, keepdims=True))
     damping = (DAMPING / order) * trace_sum
     frobenius = jnp.sqrt(squares + 2.0 * damping * trace_sum + order * damping * damping)
     scale = 1.0 / frobenius
-    power = identity - (gram + damping * identity) * scale
+    power = identity - (beside + damping * identity) * scale
     total = identity + power
-    for _ in range(NS_ITERS - 1):
-        power = split_dot(power, power)
-        total = total + split_dot(total, power)
-    return total * scale
+    for step in range(NS_ITERS):
+        high, low = halves(power)
+        right_high, right_low = spread(high), spread(low)
+        if step == 0:
+            left_high, left_low = high.astype(jnp.bfloat16), low.astype(jnp.bfloat16)
+        elif step < NS_ITERS - 1:
+            total_high, total_low = halves(total)
+            left_high = jnp.concatenate([total_high, high], axis=0).astype(jnp.bfloat16)
+            left_low = jnp.concatenate([total_low, low], axis=0).astype(jnp.bfloat16)
+        else:
+            total_high, total_low = halves(total)
+            left_high, left_low = total_high.astype(jnp.bfloat16), total_low.astype(jnp.bfloat16)
+        product = dot(left_high, right_high) + (
+            dot(left_high, right_low) + dot(left_low, right_high)
+        )
+        if step == 0:
+            power = product
+        else:
+            total = total + product[:row_count]
+            power = product[row_count:]
+    high, low = halves(total * scale)
+    return spread(high), spread(low)
 
 
 def kernel(
@@ -116,10 +152,9 @@
             pltpu.make_async_copy(out_proj_ref.at[m, span, :], out_v.at[m, c], load_sem.at[m, c, 3]),
         )
 
-    for m in range(modules):
-        for c in range(CHUNKS):
-            for copy in loads(m, c):
-                copy.start()
+    for c in range(CHUNKS):
+        for copy in loads(0, c):
+            copy.start()
 
     barrier = pltpu.get_barrier_semaphore()
 
@@ -154,11 +189,11 @@
         )
 
     def each(action):
-        def body(d, carry):
-            action(d)
+        def body(i, carry):
+            action(wide // 2 + (2 * (i % 2) - 1) * ((i + 1) // 2))
             return carry
 
-        lax.fori_loop(1, wide, body, 0)
+        lax.fori_loop(0, wide - 1, body, 0)
 
     dot = functools.partial(jnp.dot, preferred_element_type=jnp.float32)
     positions = lax.broadcasted_iota(jnp.int32, (seq_len, 1), 0)
@@ -168,6 +203,9 @@
         for c in range(CHUNKS):
             for copy in loads(m, c):
                 copy.wait()
+            if m + 1 < modules:
+                for copy in loads(m + 1, c):
+                    copy.start()
             acc_in = acc_in + dot(act_v[m, c].reshape(seqs * seq_len, depth), in_v[m, c])
             acc_out = acc_out + dot(grad_v[m, c].reshape(seqs * seq_len, depth), out_v[m, c])
         for s in range(seqs):
@@ -200,9 +238,7 @@
             ],
             axis=0,
         )
-        inverse = polynomial(stacked, blocks, BLOCK, all_seqs)
-        high = inverse.astype(jnp.bfloat16)
-        low = (inverse - high.astype(jnp.float32)).astype(jnp.bfloat16)
+        high, low = polynomial(stacked, BLOCK, all_seqs)
         solved = dot(high, stacked) + dot(low, stacked)
         for b in range(blocks):
             for j in range(lanes):
@@ -251,7 +287,7 @@
             pltpu.SemaphoreType.DMA((modules, wide)),
         ],
         compiler_params=pltpu.CompilerParams(
-            collective_id=0, has_side_effects=True, vmem_limit_bytes=40 * 1024 * 1024
+            collective_id=0, has_side_effects=True, vmem_limit_bytes=60 * 1024 * 1024
         ),
     )(lengths, activations, out_grads, proj_in, proj_out)
     return out.reshape(seqs, modules * rank_out * rank_in)

time: 41.1 us -> 36.8 us (0.90)
  local copies, waits for them, and re-layouts: 8.81 us -> 2.24 us
  Pallas kernels: 32 us -> 34.4 us
    unnamed x11 -> x1, local copies, waits for them, and re-layouts: 8.81 us -> 2.24 us
    pallas_call x1, Pallas kernels: 32 us -> 34.4 us  [local_fused(): pl.pallas_call(functools.partial(kernel, wide), out_shape=jax.ShapeDtypeS...]
where the time goes in v1:
time: 36.8 us; the launch traced here: 36.7 us
  Pallas kernels  34.4 us (93%)
  local copies, waits for them, and re-layouts  2.24 us (6%)
    pallas_call x1, Pallas kernels, local_fused(): pl.pallas_call(functools.partial(kernel, wide), out_shape=jax.ShapeDtypeS...  34.4 us
    unnamed x1, local copies, waits for them, and re-layouts  2.24 us

profile of v1, /device:TPU:0, one launch (start us, length us, event | category | flops | bytes accessed | tf_op | source)
XLA Modules:
  0.0 36.7 jit_solution(6255859341859968815)
XLA Ops:
  0.0 34.4 %shard_map.55 = bf16[4,2,256,128]{3,2,1,0:T(8,128)(2,1)} custom-call(s32[4]{0:T(128)} %lengths_ref.1, bf16[4,2,32,4096]{3,2,1,0:T(8,128)(2,1)} %act_ref.1, bf16[4,2,32,4096]{3,2,1,0:T(8,128)(2,1)} %grad_ref.1, bf16[2,4096,128]{2,1,0:T(8,128)(2,1)} %in_ref.1, bf16[2,4096,256]{2,1,0:T(8,128)(2,1)} %out_proj_ref.1), custom_call_target="tpu_custom_call" | custom-call | tf_op jit(solution)/shard_map/pallas_call | solution.py:269
  34.4 2.2 %copy.8 = bf16[1,4,512,128]{3,1,2,0:T(4,128)(2,1)} copy(bf16[1,4,512,128]{3,2,1,0:T(8,128)(2,1)} %bitcast.5) | data formatting | bytes 1048576

commit v2 on v1

--- a/solution.py
+++ b/solution.py
@@ -11,7 +11,7 @@
 BLOCK = 512
 NS_ITERS = 5
 DAMPING = 0.1
-CHUNKS = 2
+CHUNKS = 4
 MESH = pl.DeviceIdType.MESH
 
 
@@ -130,7 +130,7 @@
 
 def kernel(
     wide, lengths_ref, act_ref, grad_ref, in_ref, out_proj_ref, result_ref,
-    act_v, grad_v, in_v, out_v, outgoing, rows_v, work, finished,
+    act_v, grad_v, in_v, out_v, outgoing, rows_v, work, finished, returned,
     load_sem, send_sem, recv_sem, back_send_sem, back_recv_sem,
 ):
     seqs, modules, seq_len, width = act_ref.shape
@@ -181,7 +181,7 @@
         target = lax.rem(me + d, wide)
         return pltpu.make_async_remote_copy(
             src_ref=finished.at[m, pl.ds(target * seqs, seqs)],
-            dst_ref=result_ref.at[:, m, pl.ds(pl.multiple_of(me * here, here), here), :],
+            dst_ref=returned.at[m, me],
             send_sem=back_send_sem.at[m, d],
             recv_sem=back_recv_sem.at[m, d],
             device_id={"wide": target},
@@ -193,7 +193,7 @@
             action(wide // 2 + (2 * (i % 2) - 1) * ((i + 1) // 2))
             return carry
 
-        lax.fori_loop(0, wide - 1, body, 0)
+        lax.fori_loop(0, wide - 1, body, 0, unroll=5)
 
     dot = functools.partial(jnp.dot, preferred_element_type=jnp.float32)
     positions = lax.broadcasted_iota(jnp.int32, (seq_len, 1), 0)
@@ -247,13 +247,24 @@
                 ]
         finished[m] = work[...].astype(jnp.bfloat16).reshape(all_seqs, here, rank_in)
         each(lambda d: give_back(m, d).start())
-        result_ref[:, m, pl.ds(pl.multiple_of(me * here, here), here), :] = finished[
-            m, pl.ds(me * seqs, seqs)
-        ]
+        returned[m, me] = finished[m, pl.ds(me * seqs, seqs)]
 
     for m in range(modules):
         each(lambda d: scatter(m, d).wait_send())
         each(lambda d: give_back(m, d).wait_recv())
+        work[...] = returned[m].astype(jnp.float32).reshape(all_seqs * here, rank_in)
+
+        def place(w, carry):
+            for o in range(here):
+                start = w * (seqs * here) + o
+                lane = pl.multiple_of(((m * wide + w) * here + o) * rank_in, rank_in)
+                result_ref[:, pl.ds(lane, rank_in)] = work[
+                    pl.ds(start, seqs, stride=here), :
+                ].astype(jnp.bfloat16)
+            return carry
+
+        lax.fori_loop(0, wide, place, 0)
+    for m in range(modules):
         each(lambda d: give_back(m, d).wait_send())
 
 
@@ -266,9 +277,9 @@
     all_seqs = seqs * wide
     any_spec = pl.BlockSpec(memory_space=pl.ANY)
     bf16 = jnp.bfloat16
-    out = pl.pallas_call(
+    return pl.pallas_call(
         functools.partial(kernel, wide),
-        out_shape=jax.ShapeDtypeStruct((seqs, modules, rank_out, rank_in), bf16),
+        out_shape=jax.ShapeDtypeStruct((seqs, modules * rank_out * rank_in), bf16),
         in_specs=[pl.BlockSpec(memory_space=pltpu.SMEM)] + [any_spec] * 4,
         out_specs=pl.BlockSpec(memory_space=pltpu.VMEM),
         scratch_shapes=[
@@ -280,6 +291,7 @@
             pltpu.VMEM((modules, all_seqs, here, rank_in), bf16),
             pltpu.VMEM((all_seqs * here, rank_in), jnp.float32),
             pltpu.VMEM((modules, all_seqs, here, rank_in), bf16),
+            pltpu.VMEM((modules, wide, seqs, here, rank_in), bf16),
             pltpu.SemaphoreType.DMA((modules, CHUNKS, 4)),
             pltpu.SemaphoreType.DMA((modules, wide)),
             pltpu.SemaphoreType.DMA((modules, wide)),
@@ -287,10 +299,9 @@
             pltpu.SemaphoreType.DMA((modules, wide)),
         ],
         compiler_params=pltpu.CompilerParams(
-            collective_id=0, has_side_effects=True, vmem_limit_bytes=60 * 1024 * 1024
+            collective_id=0, has_side_effects=True, vmem_limit_bytes=58 * 1024 * 1024
         ),
     )(lengths, activations, out_grads, proj_in, proj_out)
-    return out.reshape(seqs, modules * rank_out * rank_in)
 
 
 def solution(mesh):

time: 36.8 us -> 36.6 us (level)
  no operation moved by 1% of the time
where the time goes in v2:
time: 36.6 us; the launch traced here: 36.4 us
  Pallas kernels  34.4 us (94%)
  local copies, waits for them, and re-layouts  2.02 us (6%)
    pallas_call x1, Pallas kernels, local_fused(): pl.pallas_call(functools.partial(kernel, wide), out_shape=jax.ShapeDtypeS...  34.4 us
    unnamed x1, local copies, waits for them, and re-layouts  2.02 us

profile of v2, /device:TPU:0, one launch (start us, length us, event | category | flops | bytes accessed | tf_op | source)
XLA Modules:
  0.0 36.4 jit_solution(3149635572408249483)
XLA Ops:
  0.0 34.4 %shard_map.55 = bf16[4,65536]{1,0:T(4,128)(2,1)} custom-call(s32[4]{0:T(128)} %lengths_ref.1, bf16[4,2,32,4096]{3,2,1,0:T(8,128)(2,1)} %act_ref.1, bf16[4,2,32,4096]{3,2,1,0:T(8,128)(2,1)} %grad_ref.1, bf16[2,4096,128]{2,1,0:T(8,128)(2,1)} %in_ref.1, bf16[2,4096,256]{2,1,0:T(8,128)(2,1)} %out_proj_ref.1), custom_call_target="tpu_custom_call" | custom-call | tf_op jit(solution)/shard_map/pallas_call | solution.py:280
  34.4 2.0 %copy.7 = bf16[4,65536]{1,0:T(4,128)(2,1)} copy(bf16[4,65536]{1,0:T(4,128)(2,1)} %shard_map.55) | data formatting | bytes 1048576

commit v3 on v2

--- a/solution.py
+++ b/solution.py
@@ -129,9 +129,9 @@
 
 
 def kernel(
-    wide, lengths_ref, act_ref, grad_ref, in_ref, out_proj_ref, result_ref,
-    act_v, grad_v, in_v, out_v, outgoing, rows_v, work, finished, returned,
-    load_sem, send_sem, recv_sem, back_send_sem, back_recv_sem,
+    wide, lengths_hbm, act_ref, grad_ref, in_ref, out_proj_ref, result_ref,
+    lengths_ref, act_v, grad_v, in_v, out_v, outgoing, rows_v, work, finished, returned,
+    lengths_sem, load_sem, send_sem, recv_sem, back_send_sem, back_recv_sem,
 ):
     seqs, modules, seq_len, width = act_ref.shape
     rank_in = in_ref.shape[2]
@@ -152,6 +152,8 @@
             pltpu.make_async_copy(out_proj_ref.at[m, span, :], out_v.at[m, c], load_sem.at[m, c, 3]),
         )
 
+    lengths_copy = pltpu.make_async_copy(lengths_hbm, lengths_ref, lengths_sem)
+    lengths_copy.start()
     for c in range(CHUNKS):
         for copy in loads(0, c):
             copy.start()
@@ -208,6 +210,8 @@
                     copy.start()
             acc_in = acc_in + dot(act_v[m, c].reshape(seqs * seq_len, depth), in_v[m, c])
             acc_out = acc_out + dot(grad_v[m, c].reshape(seqs * seq_len, depth), out_v[m, c])
+        if m == 0:
+            lengths_copy.wait()
         for s in range(seqs):
             valid = jnp.where(positions < lengths_ref[s], 1.0, 0.0).astype(jnp.float32)
             part = slice(s * seq_len, (s + 1) * seq_len)
@@ -275,14 +279,15 @@
     here = rank_out // wide
     depth = width // CHUNKS
     all_seqs = seqs * wide
-    any_spec = pl.BlockSpec(memory_space=pl.ANY)
+    hbm = pl.BlockSpec(memory_space=pltpu.HBM)
     bf16 = jnp.bfloat16
     return pl.pallas_call(
         functools.partial(kernel, wide),
-        out_shape=jax.ShapeDtypeStruct((seqs, modules * rank_out * rank_in), bf16),
-        in_specs=[pl.BlockSpec(memory_space=pltpu.SMEM)] + [any_spec] * 4,
+        out_shape=pltpu.VMEM((seqs, modules * rank_out * rank_in), bf16),
+        in_specs=[hbm] * 5,
         out_specs=pl.BlockSpec(memory_space=pltpu.VMEM),
         scratch_shapes=[
+            pltpu.SMEM((seqs,), jnp.int32),
             pltpu.VMEM((modules, CHUNKS, seqs, seq_len, depth), bf16),
             pltpu.VMEM((modules, CHUNKS, seqs, seq_len, depth), bf16),
             pltpu.VMEM((modules, CHUNKS, depth, rank_in), bf16),
@@ -292,6 +297,7 @@
             pltpu.VMEM((all_seqs * here, rank_in), jnp.float32),
             pltpu.VMEM((modules, all_seqs, here, rank_in), bf16),
             pltpu.VMEM((modules, wide, seqs, here, rank_in), bf16),
+            pltpu.SemaphoreType.DMA,
             pltpu.SemaphoreType.DMA((modules, CHUNKS, 4)),
             pltpu.SemaphoreType.DMA((modules, wide)),
             pltpu.SemaphoreType.DMA((modules, wide)),

time: 36.6 us -> 33.9 us (0.926)
  Pallas kernels: 34.4 us -> 33 us
  local copies, waits for them, and re-layouts: 2.02 us -> 0.8 us
    pallas_call x1, Pallas kernels: 34.4 us -> 33 us  [local_fused(): pl.pallas_call(functools.partial(kernel, wide), out_shape=pltpu.VMEM((seq...]
    unnamed x1, local copies, waits for them, and re-layouts: 2.02 us -> 0.8 us
where the time goes in v3:
time: 33.9 us; the launch traced here: 33.8 us
  Pallas kernels  33 us (97%)
  local copies, waits for them, and re-layouts  0.8 us (2%)
    pallas_call x1, Pallas kernels, local_fused(): pl.pallas_call(functools.partial(kernel, wide), out_shape=pltpu.VMEM((seq...  33 us
    unnamed x1, local copies, waits for them, and re-layouts  0.8 us

profile of v3, /device:TPU:0, one launch (start us, length us, event | category | flops | bytes accessed | tf_op | source)
XLA Modules:
  0.0 33.8 jit_solution(9614577785422501715)
XLA Ops:
  0.0 33.0 %shard_map.55 = bf16[4,65536]{1,0:T(4,128)(2,1)S(1)} custom-call(s32[4]{0:T(128)} %lengths_hbm.1, bf16[4,2,32,4096]{3,2,1,0:T(8,128)(2,1)} %act_ref.1, bf16[4,2,32,4096]{3,2,1,0:T(8,128)(2,1)} %grad_ref.1, bf16[2,4096,128]{2,1,0:T(8,128)(2,1)} %in_ref.1, bf16[2,4096,256]{2,1,0:T(8,128)(2,1)} %out_proj_ref.1), custom_call_target="tpu_custom_call" | custom-call | tf_op jit(solution)/shard_map/pallas_call | solution.py:284
  33.0 0.8 %copy.7 = bf16[4,65536]{1,0:T(4,128)(2,1)} copy(bf16[4,65536]{1,0:T(4,128)(2,1)S(1)} %shard_map.55) | data formatting | bytes 1048576

commit v4 on v3

--- a/solution.py
+++ b/solution.py
@@ -130,33 +130,45 @@
 
 def kernel(
     wide, lengths_hbm, act_ref, grad_ref, in_ref, out_proj_ref, result_ref,
-    lengths_ref, act_v, grad_v, in_v, out_v, outgoing, rows_v, work, finished, returned,
+    lengths_ref, act_v, grad_v, in_v, out_v, inputs, outgoing, incoming, work, finished, returned,
     lengths_sem, load_sem, send_sem, recv_sem, back_send_sem, back_recv_sem,
+    far_send_sem, far_recv_sem, pair_send_sem, pair_recv_sem, core_send_sem, core_recv_sem,
 ):
     seqs, modules, seq_len, width = act_ref.shape
     rank_in = in_ref.shape[2]
     rank_out = out_proj_ref.shape[2]
     here = rank_out // wide
+    tokens = seqs * seq_len
     all_seqs = seqs * wide
     lanes = BLOCK // rank_in
     blocks = here // lanes
     depth = width // CHUNKS
+    quads = wide // 4
     me = lax.axis_index("wide")
-
-    def loads(m, c):
+    quad, rank = me // 4, lax.rem(me, 4)
+    pair_rank = lax.rem(rank + 2, 4)
+    sibling = me + 1 - 2 * lax.rem(me, 2)
+
+    def loads(m, side, c):
         span = pl.ds(c * depth, depth)
+        source, projector = ((act_ref, in_ref), (grad_ref, out_proj_ref))[side]
+        source_v, projector_v = ((act_v, in_v), (grad_v, out_v))[side]
         return (
-            pltpu.make_async_copy(act_ref.at[:, m, :, span], act_v.at[m, c], load_sem.at[m, c, 0]),
-            pltpu.make_async_copy(in_ref.at[m, span, :], in_v.at[m, c], load_sem.at[m, c, 1]),
-            pltpu.make_async_copy(grad_ref.at[:, m, :, span], grad_v.at[m, c], load_sem.at[m, c, 2]),
-            pltpu.make_async_copy(out_proj_ref.at[m, span, :], out_v.at[m, c], load_sem.at[m, c, 3]),
-        )
-
+            pltpu.make_async_copy(
+                source.at[:, m, :, span], source_v.at[m, c], load_sem.at[m, c, 2 * side]
+            ),
+            pltpu.make_async_copy(
+                projector.at[m, span, :], projector_v.at[m, c], load_sem.at[m, c, 2 * side + 1]
+            ),
+        )
+
+    stages = [(m, side) for m in range(modules) for side in range(2)]
     lengths_copy = pltpu.make_async_copy(lengths_hbm, lengths_ref, lengths_sem)
     lengths_copy.start()
-    for c in range(CHUNKS):
-        for copy in loads(0, c):
-            copy.start()
+    for stage in stages[:2]:
+        for c in range(CHUNKS):
+            for copy in loads(*stage, c):
+                copy.start()
 
     barrier = pltpu.get_barrier_semaphore()
 
@@ -167,12 +179,37 @@
         return carry
 
     lax.fori_loop(1, wide, greet, 0)
+
+    def hand(m, slot, target, send, recv):
+        return pltpu.make_async_remote_copy(
+            src_ref=inputs.at[m, slot],
+            dst_ref=inputs.at[m, slot],
+            send_sem=send,
+            recv_sem=recv,
+            device_id={"wide": target},
+            device_id_type=MESH,
+        )
+
+    def origin(k, of_rank):
+        return lax.rem(quad + quads - k, quads) * 4 + of_rank
+
+    def to_quad(m, j):
+        target = lax.rem(quad + j, quads) * 4 + rank
+        return hand(m, me, target, far_send_sem.at[m, j], far_recv_sem.at[m, j])
+
+    def to_pair(m, k):
+        target = quad * 4 + pair_rank
+        return hand(m, origin(k, rank), target, pair_send_sem.at[m, k], pair_recv_sem.at[m, k])
+
+    def to_core(m, k):
+        slot = origin(k, rank) if k < quads else origin(k - quads, pair_rank)
+        return hand(m, slot, sibling, core_send_sem.at[m, k], core_recv_sem.at[m, k])
 
     def scatter(m, d):
         target = lax.rem(me + d, wide)
         return pltpu.make_async_remote_copy(
             src_ref=outgoing.at[m, target],
-            dst_ref=rows_v.at[m, pl.ds(me * seqs, seqs)],
+            dst_ref=incoming.at[m, me],
             send_sem=send_sem.at[m, d],
             recv_sem=recv_sem.at[m, d],
             device_id={"wide": target},
@@ -197,38 +234,68 @@
 
         lax.fori_loop(0, wide - 1, body, 0, unroll=5)
 
+    def hand_on(m):
+        for j in range(1, quads):
+            to_quad(m, j).wait_recv()
+            to_pair(m, j).start()
+            to_core(m, j).start()
+
     dot = functools.partial(jnp.dot, preferred_element_type=jnp.float32)
     positions = lax.broadcasted_iota(jnp.int32, (seq_len, 1), 0)
+
+    def valid():
+        return jnp.concatenate(
+            [
+                jnp.where(positions < lengths_ref[s], 1.0, 0.0).astype(jnp.float32)
+                for s in range(seqs)
+            ],
+            axis=0,
+        )
+
+    for index, (m, side) in enumerate(stages):
+        source_v, projector_v = ((act_v, in_v), (grad_v, out_v))[side]
+        total = jnp.zeros((tokens, (rank_in, rank_out)[side]), jnp.float32)
+        for c in range(CHUNKS):
+            for copy in loads(m, side, c):
+                copy.wait()
+            if index + 2 < len(stages):
+                for copy in loads(*stages[index + 2], c):
+                    copy.start()
+            total = total + dot(source_v[m, c].reshape(tokens, depth), projector_v[m, c])
+        if index == 0:
+            lengths_copy.wait()
+        total = total * valid()
+        if side == 0:
+            inputs[m, me] = total.astype(jnp.bfloat16)
+            if index == 0:
+                pl.semaphore_wait(barrier, wide - 1)
+            for j in range(1, quads):
+                to_quad(m, j).start()
+            to_pair(m, 0).start()
+            to_core(m, 0).start()
+        else:
+            outgoing[m] = total.T.astype(jnp.bfloat16).reshape(wide, here, tokens)
+            each(lambda d: scatter(m, d).start())
+            incoming[m, me] = outgoing[m, me]
+
+    own_tokens = (
+        lax.broadcasted_iota(jnp.int32, (seqs * here, tokens), 0) // here
+        == lax.broadcasted_iota(jnp.int32, (seqs * here, tokens), 1) // seq_len
+    )
+    hand_on(0)
     for m in range(modules):
-        acc_in = jnp.zeros((seqs * seq_len, rank_in), jnp.float32)
-        acc_out = jnp.zeros((seqs * seq_len, rank_out), jnp.float32)
-        for c in range(CHUNKS):
-            for copy in loads(m, c):
-                copy.wait()
-            if m + 1 < modules:
-                for copy in loads(m + 1, c):
-                    copy.start()
-            acc_in = acc_in + dot(act_v[m, c].reshape(seqs * seq_len, depth), in_v[m, c])
-            acc_out = acc_out + dot(grad_v[m, c].reshape(seqs * seq_len, depth), out_v[m, c])
-        if m == 0:
-            lengths_copy.wait()
-        for s in range(seqs):
-            valid = jnp.where(positions < lengths_ref[s], 1.0, 0.0).astype(jnp.float32)
-            part = slice(s * seq_len, (s + 1) * seq_len)
-            left = (acc_out[part] * valid).astype(jnp.bfloat16)
-            right = (acc_in[part] * valid).astype(jnp.bfloat16)
-            product = lax.dot_general(
-                left, right, (((0,), (0,)), ((), ())), preferred_element_type=jnp.float32
-            ) * (1.0 / math.sqrt(seq_len))
-            outgoing[m, :, s] = product.astype(jnp.bfloat16).reshape(wide, here, rank_in)
-        if m == 0:
-            pl.semaphore_wait(barrier, wide - 1)
-        each(lambda d: scatter(m, d).start())
-        rows_v[m, pl.ds(me * seqs, seqs)] = outgoing[m, me]
-
-    for m in range(modules):
+        for k in range(quads):
+            to_pair(m, k).wait_recv()
+            to_core(m, quads + k).start()
         each(lambda d: scatter(m, d).wait_recv())
-        work[...] = rows_v[m].astype(jnp.float32).reshape(all_seqs * here, rank_in)
+        for k in range(2 * quads):
+            to_core(m, k).wait_recv()
+        for w in range(wide):
+            left = jnp.concatenate([incoming[m, w].astype(jnp.float32)] * seqs, axis=0)
+            left = jnp.where(own_tokens, left, 0.0).astype(jnp.bfloat16)
+            work[w * seqs * here : (w + 1) * seqs * here, :] = dot(left, inputs[m, w]) * (
+                1.0 / math.sqrt(seq_len)
+            )
         stacked = jnp.concatenate(
             [
                 jnp.concatenate(
@@ -244,6 +311,8 @@
         )
         high, low = polynomial(stacked, BLOCK, all_seqs)
         solved = dot(high, stacked) + dot(low, stacked)
+        if m + 1 < modules:
+            hand_on(m + 1)
         for b in range(blocks):
             for j in range(lanes):
                 work[pl.ds(b * lanes + j, all_seqs, stride=here), :] = solved[
@@ -255,6 +324,12 @@
 
     for m in range(modules):
         each(lambda d: scatter(m, d).wait_send())
+        for j in range(1, quads):
+            to_quad(m, j).wait_send()
+        for k in range(quads):
+            to_pair(m, k).wait_send()
+        for k in range(2 * quads):
+            to_core(m, k).wait_send()
         each(lambda d: give_back(m, d).wait_recv())
         work[...] = returned[m].astype(jnp.float32).reshape(all_seqs * here, rank_in)
 
@@ -292,8 +367,9 @@
             pltpu.VMEM((modules, CHUNKS, seqs, seq_len, depth), bf16),
             pltpu.VMEM((modules, CHUNKS, depth, rank_in), bf16),
             pltpu.VMEM((modules, CHUNKS, depth, rank_out), bf16),
-            pltpu.VMEM((modules, wide, seqs, here, rank_in), bf16),
-            pltpu.VMEM((modules, all_seqs, here, rank_in), bf16),
+            pltpu.VMEM((modules, wide, seqs * seq_len, rank_in), bf16),
+            pltpu.VMEM((modules, wide, here, seqs * seq_len), bf16),
+            pltpu.VMEM((modules, wide, here, seqs * seq_len), bf16),
             pltpu.VMEM((all_seqs * here, rank_in), jnp.float32),
             pltpu.VMEM((modules, all_seqs, here, rank_in), bf16),
             pltpu.VMEM((modules, wide, seqs, here, rank_in), bf16),
@@ -303,6 +379,12 @@
             pltpu.SemaphoreType.DMA((modules, wide)),
             pltpu.SemaphoreType.DMA((modules, wide)),
             pltpu.SemaphoreType.DMA((modules, wide)),
+            pltpu.SemaphoreType.DMA((modules, wide // 4)),
+            pltpu.SemaphoreType.DMA((modules, wide // 4)),
+            pltpu.SemaphoreType.DMA((modules, wide // 4)),
+            pltpu.SemaphoreType.DMA((modules, wide // 4)),
+            pltpu.SemaphoreType.DMA((modules, wide // 2)),
+            pltpu.SemaphoreType.DMA((modules, wide // 2)),
         ],
         compiler_params=pltpu.CompilerParams(
             collective_id=0, has_side_effects=True, vmem_limit_bytes=58 * 1024 * 1024
@@ -325,7 +407,9 @@
         here = proj_out.shape[2] // wide
         lanes = BLOCK // proj_in.shape[2]
         stacked = activations.shape[0] * wide * max(here // lanes, 1)
-        if here % 16 == 0 and here % lanes == 0 and stacked <= 512:
+        tokens = activations.shape[0] * activations.shape[2]
+        whole_tiles = here % 16 == 0 and here % lanes == 0 and tokens % 128 == 0
+        if whole_tiles and wide % 4 == 0 and stacked <= 512:
             return local_fused(wide, activations, out_grads, lengths, proj_in, proj_out)
         return local_plain(activations, out_grads, lengths, proj_in, proj_out)
 

time: 33.9 us -> 37 us (1.091)
  Pallas kernels: 33 us -> 36 us
    pallas_call x1, Pallas kernels: 33 us -> 36 us  [local_fused(): pl.pallas_call(functools.partial(kernel, wide), out_shape=pltpu.VMEM((seq...]
where the time goes in v4:
time: 37 us; the launch traced here: 36.8 us
  Pallas kernels  36 us (97%)
  local copies, waits for them, and re-layouts  0.8 us (2%)
    pallas_call x1, Pallas kernels, local_fused(): pl.pallas_call(functools.partial(kernel, wide), out_shape=pltpu.VMEM((seq...  36 us
    unnamed x1, local copies, waits for them, and re-layouts  0.8 us

profile of v4, /device:TPU:0, one launch (start us, length us, event | category | flops | bytes accessed | tf_op | source)
XLA Modules:
  0.0 36.8 jit_solution(14205675260709516957)
XLA Ops:
  0.0 36.0 %shard_map.55 = bf16[4,65536]{1,0:T(4,128)(2,1)S(1)} custom-call(s32[4]{0:T(128)} %lengths_hbm.1, bf16[4,2,32,4096]{3,2,1,0:T(8,128)(2,1)} %act_ref.1, bf16[4,2,32,4096]{3,2,1,0:T(8,128)(2,1)} %grad_ref.1, bf16[2,4096,128]{2,1,0:T(8,128)(2,1)} %in_ref.1, bf16[2,4096,256]{2,1,0:T(8,128)(2,1)} %out_proj_ref.1), custom_call_target="tpu_custom_call" | custom-call | tf_op jit(solution)/shard_map/pallas_call | solution.py:359
  36.0 0.8 %copy.7 = bf16[4,65536]{1,0:T(4,128)(2,1)} copy(bf16[4,65536]{1,0:T(4,128)(2,1)S(1)} %shard_map.55) | data formatting | bytes 1048576

commit v5 on v3

--- a/solution.py
+++ b/solution.py
@@ -166,15 +166,15 @@
         )
         return carry
 
-    lax.fori_loop(1, wide, greet, 0)
+    lax.fori_loop(1, wide, greet, 0, unroll=5)
 
     def scatter(m, d):
         target = lax.rem(me + d, wide)
         return pltpu.make_async_remote_copy(
             src_ref=outgoing.at[m, target],
             dst_ref=rows_v.at[m, pl.ds(me * seqs, seqs)],
-            send_sem=send_sem.at[m, d],
-            recv_sem=recv_sem.at[m, d],
+            send_sem=send_sem.at[m],
+            recv_sem=recv_sem.at[m],
             device_id={"wide": target},
             device_id_type=MESH,
         )
@@ -184,9 +184,20 @@
         return pltpu.make_async_remote_copy(
             src_ref=finished.at[m, pl.ds(target * seqs, seqs)],
             dst_ref=returned.at[m, me],
-            send_sem=back_send_sem.at[m, d],
+            send_sem=back_send_sem.at[m],
             recv_sem=back_recv_sem.at[m, d],
             device_id={"wide": target},
+            device_id_type=MESH,
+        )
+
+    def all_others(buffer, m, send, recv):
+        part = buffer.at[m, pl.ds(0, (wide - 1) * seqs)]
+        return pltpu.make_async_remote_copy(
+            src_ref=part,
+            dst_ref=part,
+            send_sem=send,
+            recv_sem=recv,
+            device_id={"wide": lax.rem(me + 1, wide)},
             device_id_type=MESH,
         )
 
@@ -227,7 +238,7 @@
         rows_v[m, pl.ds(me * seqs, seqs)] = outgoing[m, me]
 
     for m in range(modules):
-        each(lambda d: scatter(m, d).wait_recv())
+        all_others(rows_v, m, send_sem.at[m], recv_sem.at[m]).wait_recv()
         work[...] = rows_v[m].astype(jnp.float32).reshape(all_seqs * here, rank_in)
         stacked = jnp.concatenate(
             [
@@ -253,23 +264,30 @@
         each(lambda d: give_back(m, d).start())
         returned[m, me] = finished[m, pl.ds(me * seqs, seqs)]
 
-    for m in range(modules):
-        each(lambda d: scatter(m, d).wait_send())
-        each(lambda d: give_back(m, d).wait_recv())
-        work[...] = returned[m].astype(jnp.float32).reshape(all_seqs * here, rank_in)
-
-        def place(w, carry):
-            for o in range(here):
-                start = w * (seqs * here) + o
-                lane = pl.multiple_of(((m * wide + w) * here + o) * rank_in, rank_in)
-                result_ref[:, pl.ds(lane, rank_in)] = work[
-                    pl.ds(start, seqs, stride=here), :
-                ].astype(jnp.bfloat16)
+    def place(m, w):
+        rows = seqs * here
+        top = pl.multiple_of(w * rows, rows)
+        work[pl.ds(top, rows), :] = returned[m, w].astype(jnp.float32).reshape(rows, rank_in)
+        for o in range(here):
+            lane = pl.multiple_of(((m * wide + w) * here + o) * rank_in, rank_in)
+            result_ref[:, pl.ds(lane, rank_in)] = work[
+                pl.ds(top + o, seqs, stride=here), :
+            ].astype(jnp.bfloat16)
+
+    for m in range(modules):
+        all_others(rows_v, m, send_sem.at[m], recv_sem.at[m]).wait_send()
+        place(m, me)
+    for m in range(modules):
+
+        def take(i, carry):
+            d = wide // 2 + (2 * (i % 2) - 1) * ((i + 1) // 2)
+            give_back(m, d).wait_recv()
+            place(m, lax.rem(me + wide - d, wide))
             return carry
 
-        lax.fori_loop(0, wide, place, 0)
-    for m in range(modules):
-        each(lambda d: give_back(m, d).wait_send())
+        lax.fori_loop(0, wide - 1, take, 0)
+    for m in range(modules):
+        all_others(finished, m, back_send_sem.at[m], recv_sem.at[m]).wait_send()
 
 
 def local_fused(wide, activations, out_grads, lengths, proj_in, proj_out):
@@ -299,9 +317,9 @@
             pltpu.VMEM((modules, wide, seqs, here, rank_in), bf16),
             pltpu.SemaphoreType.DMA,
             pltpu.SemaphoreType.DMA((modules, CHUNKS, 4)),
-            pltpu.SemaphoreType.DMA((modules, wide)),
-            pltpu.SemaphoreType.DMA((modules, wide)),
-            pltpu.SemaphoreType.DMA((modules, wide)),
+            pltpu.SemaphoreType.DMA((modules,)),
+            pltpu.SemaphoreType.DMA((modules,)),
+            pltpu.SemaphoreType.DMA((modules,)),
             pltpu.SemaphoreType.DMA((modules, wide)),
         ],
         compiler_params=pltpu.CompilerParams(

time: 33.9 us -> 32.7 us (0.965)
  Pallas kernels: 33 us -> 31.7 us
    pallas_call x1, Pallas kernels: 33 us -> 31.7 us  [local_fused(): pl.pallas_call(functools.partial(kernel, wide), out_shape=pltpu.VMEM((seq...]
where the time goes in v5:
time: 32.7 us; the launch traced here: 32.5 us
  Pallas kernels  31.7 us (97%)
  local copies, waits for them, and re-layouts  0.8 us (2%)
    pallas_call x1, Pallas kernels, local_fused(): pl.pallas_call(functools.partial(kernel, wide), out_shape=pltpu.VMEM((seq...  31.7 us
    unnamed x1, local copies, waits for them, and re-layouts  0.8 us

profile of v5, /device:TPU:0, one launch (start us, length us, event | category | flops | bytes accessed | tf_op | source)
XLA Modules:
  0.0 32.5 jit_solution(10838834844907224050)
XLA Ops:
  0.0 31.7 %shard_map.55 = bf16[4,65536]{1,0:T(4,128)(2,1)S(1)} custom-call(s32[4]{0:T(128)} %lengths_hbm.1, bf16[4,2,32,4096]{3,2,1,0:T(8,128)(2,1)} %act_ref.1, bf16[4,2,32,4096]{3,2,1,0:T(8,128)(2,1)} %grad_ref.1, bf16[2,4096,128]{2,1,0:T(8,128)(2,1)} %in_ref.1, bf16[2,4096,256]{2,1,0:T(8,128)(2,1)} %out_proj_ref.1), custom_call_target="tpu_custom_call" | custom-call | tf_op jit(solution)/shard_map/pallas_call | solution.py:302
  31.7 0.8 %copy.7 = bf16[4,65536]{1,0:T(4,128)(2,1)} copy(bf16[4,65536]{1,0:T(4,128)(2,1)S(1)} %shard_map.55) | data formatting | bytes 1048576

commit v6 on v5

--- a/solution.py
+++ b/solution.py
@@ -58,23 +58,26 @@
     return returned.reshape(seq_count, grad_size)
 
 
-def polynomial(stacked, order, row_count):
-    size = stacked.shape[0]
-    blocks = size // row_count
+def block_masks(size, row_count):
     row = lax.broadcasted_iota(jnp.int32, (size, size), 0)
     column = lax.broadcasted_iota(jnp.int32, (size, size), 1)
-    same = row // row_count == column // row_count
+    mask = jnp.where(row // row_count == column // row_count, 1.0, 0.0).astype(jnp.bfloat16)
     short = (row_count, size)
-    lane = lax.broadcasted_iota(jnp.int32, (1, size), 1)
     on_diagonal = (
         lax.broadcasted_iota(jnp.int32, short, 0)
         == lax.broadcasted_iota(jnp.int32, short, 1) % row_count
     )
-    identity = jnp.where(on_diagonal, 1.0, 0.0).astype(jnp.float32)
+    return mask, jnp.where(on_diagonal, 1.0, 0.0).astype(jnp.float32)
+
+
+def polynomial(stacked, order, row_count, masks):
+    size = stacked.shape[0]
+    blocks = size // row_count
+    mask, identity = masks
+    lane = lax.broadcasted_iota(jnp.int32, (1, size), 1)
 
     def spread(beside):
-        tall = jnp.concatenate([beside] * blocks, axis=0)
-        return jnp.where(same, tall, 0.0).astype(jnp.bfloat16)
+        return jnp.concatenate([beside.astype(jnp.bfloat16)] * blocks, axis=0) * mask
 
     def halves(beside):
         high = beside.astype(jnp.bfloat16).astype(jnp.float32)
@@ -92,10 +95,10 @@
     gram = lax.dot_general(
         stacked, stacked, (((1,), (1,)), ((), ())), preferred_element_type=jnp.float32
     )
-    gram = jnp.where(same, gram, 0.0)
     beside = gram[:row_count]
     for b in range(1, blocks):
-        beside = beside + gram[b * row_count : (b + 1) * row_count]
+        mine = lane // row_count == b
+        beside = jnp.where(mine, gram[b * row_count : (b + 1) * row_count], beside)
     beside = beside * (1.0 / row_count)
     trace_sum = per_block(jnp.sum(beside * identity, axis=0, keepdims=True))
     squares = per_block(jnp.sum(beside * beside, axis=0, keepdims=True))
@@ -237,6 +240,12 @@
         each(lambda d: scatter(m, d).start())
         rows_v[m, pl.ds(me * seqs, seqs)] = outgoing[m, me]
 
+    def rounded(w):
+        rows = seqs * here
+        part = work[pl.ds(pl.multiple_of(w * rows, rows), rows), :]
+        return part.astype(jnp.bfloat16).reshape(seqs, here, rank_in)
+
+    masks = block_masks(blocks * all_seqs, all_seqs)
     for m in range(modules):
         all_others(rows_v, m, send_sem.at[m], recv_sem.at[m]).wait_recv()
         work[...] = rows_v[m].astype(jnp.float32).reshape(all_seqs * here, rank_in)
@@ -253,16 +262,20 @@
             ],
             axis=0,
         )
-        high, low = polynomial(stacked, BLOCK, all_seqs)
+        high, low = polynomial(stacked, BLOCK, all_seqs, masks)
         solved = dot(high, stacked) + dot(low, stacked)
         for b in range(blocks):
             for j in range(lanes):
                 work[pl.ds(b * lanes + j, all_seqs, stride=here), :] = solved[
                     b * all_seqs : (b + 1) * all_seqs, j * rank_in : (j + 1) * rank_in
                 ]
-        finished[m] = work[...].astype(jnp.bfloat16).reshape(all_seqs, here, rank_in)
-        each(lambda d: give_back(m, d).start())
-        returned[m, me] = finished[m, pl.ds(me * seqs, seqs)]
+
+        def answer(d):
+            finished[m, pl.ds(lax.rem(me + d, wide) * seqs, seqs)] = rounded(lax.rem(me + d, wide))
+            give_back(m, d).start()
+
+        each(answer)
+        returned[m, me] = rounded(me)
 
     def place(m, w):
         rows = seqs * here

time: 32.7 us -> 32.7 us (level)
  no operation moved by 1% of the time
where the time goes in v6:
time: 32.7 us; the launch traced here: 32.5 us
  Pallas kernels  31.7 us (97%)
  local copies, waits for them, and re-layouts  0.8 us (2%)
    pallas_call x1, Pallas kernels, local_fused(): pl.pallas_call(functools.partial(kernel, wide), out_shape=pltpu.VMEM((seq...  31.7 us
    unnamed x1, local copies, waits for them, and re-layouts  0.8 us

profile of v6, /device:TPU:0, one launch (start us, length us, event | category | flops | bytes accessed | tf_op | source)
XLA Modules:
  0.0 32.5 jit_solution(11754238116496174945)
XLA Ops:
  0.0 31.7 %shard_map.55 = bf16[4,65536]{1,0:T(4,128)(2,1)S(1)} custom-call(s32[4]{0:T(128)} %lengths_hbm.1, bf16[4,2,32,4096]{3,2,1,0:T(8,128)(2,1)} %act_ref.1, bf16[4,2,32,4096]{3,2,1,0:T(8,128)(2,1)} %grad_ref.1, bf16[2,4096,128]{2,1,0:T(8,128)(2,1)} %in_ref.1, bf16[2,4096,256]{2,1,0:T(8,128)(2,1)} %out_proj_ref.1), custom_call_target="tpu_custom_call" | custom-call | tf_op jit(solution)/shard_map/pallas_call | solution.py:315
  31.7 0.8 %copy.7 = bf16[4,65536]{1,0:T(4,128)(2,1)} copy(bf16[4,65536]{1,0:T(4,128)(2,1)S(1)} %shard_map.55) | data formatting | bytes 1048576

commit v7 on v6

--- a/solution.py
+++ b/solution.py
@@ -206,7 +206,7 @@
 
     def each(action):
         def body(i, carry):
-            action(wide // 2 + (2 * (i % 2) - 1) * ((i + 1) // 2))
+            action(lax.rem((i + 1) * (wide // 2 - 1), wide))
             return carry
 
         lax.fori_loop(0, wide - 1, body, 0, unroll=5)
@@ -293,7 +293,7 @@
     for m in range(modules):
 
         def take(i, carry):
-            d = wide // 2 + (2 * (i % 2) - 1) * ((i + 1) // 2)
+            d = lax.rem((i + 1) * (wide // 2 - 1), wide)
             give_back(m, d).wait_recv()
             place(m, lax.rem(me + wide - d, wide))
             return carry
@@ -356,7 +356,7 @@
         here = proj_out.shape[2] // wide
         lanes = BLOCK // proj_in.shape[2]
         stacked = activations.shape[0] * wide * max(here // lanes, 1)
-        if here % 16 == 0 and here % lanes == 0 and stacked <= 512:
+        if wide % 4 == 0 and here % 16 == 0 and here % lanes == 0 and stacked <= 512:
             return local_fused(wide, activations, out_grads, lengths, proj_in, proj_out)
         return local_plain(activations, out_grads, lengths, proj_in, proj_out)
 

time: 32.7 us -> 32.5 us (level)
  no operation moved by 1% of the time
where the time goes in v7:
time: 32.5 us; the launch traced here: 32.3 us
  Pallas kernels  31.5 us (97%)
  local copies, waits for them, and re-layouts  0.8 us (2%)
    pallas_call x1, Pallas kernels, local_fused(): pl.pallas_call(functools.partial(kernel, wide), out_shape=pltpu.VMEM((seq...  31.5 us
    unnamed x1, local copies, waits for them, and re-layouts  0.8 us

profile of v7, /device:TPU:0, one launch (start us, length us, event | category | flops | bytes accessed | tf_op | source)
XLA Modules:
  0.0 32.3 jit_solution(11168127600508747455)
XLA Ops:
  0.0 31.5 %shard_map.55 = bf16[4,65536]{1,0:T(4,128)(2,1)S(1)} custom-call(s32[4]{0:T(128)} %lengths_hbm.1, bf16[4,2,32,4096]{3,2,1,0:T(8,128)(2,1)} %act_ref.1, bf16[4,2,32,4096]{3,2,1,0:T(8,128)(2,1)} %grad_ref.1, bf16[2,4096,128]{2,1,0:T(8,128)(2,1)} %in_ref.1, bf16[2,4096,256]{2,1,0:T(8,128)(2,1)} %out_proj_ref.1), custom_call_target="tpu_custom_call" | custom-call | tf_op jit(solution)/shard_map/pallas_call | solution.py:315
  31.5 0.8 %copy.7 = bf16[4,65536]{1,0:T(4,128)(2,1)} copy(bf16[4,65536]{1,0:T(4,128)(2,1)S(1)} %shard_map.55) | data formatting | bytes 1048576
